TPU v7x, 32 devices: a whole 2x2x4 slice. The times are simulated.
32 devices in a mesh: sec: 2 (over x), blk: 8 (over z, y), head: 2 (over core).
Axes of the slice: x: 2, y: 2, z: 4, core: 2. Of those that a mesh axis runs over, the one named last changes fastest.
Arguments:
- tokens: bfloat16 [8192, 768], P(('sec', 'blk')), parts along dimension 0, may hold values from -6 to 6
- counts: int32 [16], P(('sec', 'blk')), parts along dimension 0, may hold values from 128 to 512, as said below
- face_owner: int32 [6, 8192], P(None, ('sec', 'blk')), parts along dimension 1, may hold values from 0 to 7, as said below
- face_row: int32 [6, 8192], P(None, ('sec', 'blk')), parts along dimension 1, may hold values from 0 to 511, as said below
- face_count: int32 [8192], P(('sec', 'blk')), parts along dimension 0, may hold values from 1 to 6
- mix_weight: bfloat16 [768, 768], P(None, 'head'), may hold values from -0.21875 to 0.21875
- norm_gain: bfloat16 [768], replicated, may hold values from 0.25 to 1.75
- query_weight: bfloat16 [768, 768], P(None, 'head'), may hold values from -1 to 1
- key_weight: bfloat16 [768, 768], P(None, 'head'), may hold values from -1 to 1
- value_weight: bfloat16 [768, 768], P(None, 'head'), may hold values from -0.21875 to 0.21875
- out_weight: bfloat16 [768, 768], P('head'), may hold values from -0.21875 to 0.21875
Outputs:
- layer_out: bfloat16 [8192, 768], P(('sec', 'blk'), 'head'), parts along dimension 0
There are 2 independent parts, one for each index of `sec`. A program takes and returns all parts, laid end to end along the dimension named above; an argument that names none is the same for every part. Nothing has to cross between parts.
Inputs may be any that keep to these rules, and one draw needn't show every extreme that they name: `counts`: each section has one block with exactly 512 live tokens and one with exactly 128. `face_owner`: A token's face neighbours lie in its own block or in the blocks one index below or above it, the last block's above being block 0. `face_row`: A face neighbour is a live slot of its owner's block.
All inputs are finite; a program needn't handle non-finite values.
Results may differ from a plain program's by a relative error of at most 0.012.
The roundings to bfloat16 on the way count: a program that leaves them out, or rounds other values in their place, can miss the bound.
Values may be sent and summed in bfloat16 or wider, within the bound.
A program may use at most 64 MiB of HBM per device.

v0:
```python
import jax
import jax.numpy as jnp
from jax import lax
from jax.sharding import PartitionSpec as P

HS = 64


def extended_2(array, sides, width):
    for axis, dim in sides:
        size, length = (lax.axis_size(axis), array.shape[dim])
        up = [(i, (i + 1) % size) for i in range(size)]
        down = [(j, i) for i, j in up]
        last = lax.slice_in_dim(array, length - width, length, axis=dim)
        first = lax.slice_in_dim(array, 0, width, axis=dim)
        before = lax.ppermute(last, axis, up)
        after = lax.ppermute(first, axis, down)
        array = jnp.concatenate([before, array, after], axis=dim)
    return array


def rms_norm(values, gain):
    var = jnp.mean(values * values, axis=-1, keepdims=True)
    return values * lax.rsqrt(var + 1e-05) * gain


def local(
    tokens,
    counts,
    face_owner,
    face_row,
    face_count,
    mix_weight,
    norm_gain,
    query_weight,
    key_weight,
    value_weight,
    out_weight,
):
    rows = tokens.shape[0]
    faces = face_owner.shape[0]
    cycle_size = lax.axis_size("blk")
    place = lax.axis_index("blk")
    half = mix_weight.shape[1]
    head_place = lax.axis_index("head")
    extended = extended_2(tokens, (("blk", 0),), rows)
    offset = (face_owner - place + 1 + cycle_size) % cycle_size
    local_rows = offset * rows + face_row
    picked = extended[local_rows]
    live = lax.broadcasted_iota(jnp.int32, (faces, rows), 0) < face_count[None, :]
    picked = jnp.where(live[:, :, None], picked, jnp.zeros((), jnp.bfloat16))
    summed = jnp.sum(picked, axis=0, dtype=jnp.float32)
    summed = (summed / face_count[:, None].astype(jnp.float32)).astype(jnp.bfloat16)
    own_tokens = lax.dynamic_slice_in_dim(tokens, head_place * half, half, 1)
    own_mixed = own_tokens.astype(jnp.float32) + jnp.dot(
        summed, mix_weight, preferred_element_type=jnp.float32
    )
    stream = lax.all_gather(own_mixed.astype(jnp.bfloat16), "head", axis=1, tiled=True)
    normed = rms_norm(stream.astype(jnp.float32), norm_gain.astype(jnp.float32)).astype(
        jnp.bfloat16
    )
    heads = query_weight.shape[1] // HS
    scale = 1.0 / HS**0.5
    query = jnp.dot(normed, query_weight, preferred_element_type=jnp.float32).astype(jnp.bfloat16)
    query_heads = query.reshape(rows, heads, HS)

    def attend_block(carry, block):
        top, total, acc = carry
        keys, values, live_count = block
        key_heads = keys.reshape(rows, heads, HS)
        value_heads = values.reshape(rows, heads, HS)
        key_live = lax.broadcasted_iota(jnp.int32, (rows,), 0) < live_count
        scores = (
            jnp.einsum("qhd,khd->hqk", query_heads, key_heads, preferred_element_type=jnp.float32)
            * scale
        )
        scores = jnp.where(key_live[None, None, :], scores, -1e30)
        new_top = jnp.maximum(top, jnp.max(scores, axis=-1))
        fade = jnp.exp(top - new_top)
        probs = jnp.where(key_live[None, None, :], jnp.exp(scores - new_top[:, :, None]), 0.0)
        total = total * fade + jnp.sum(probs, axis=-1)
        update = jnp.einsum(
            "hqk,khd->hqd",
            probs.astype(jnp.bfloat16),
            value_heads,
            preferred_element_type=jnp.float32,
        )
        acc = acc * fade[:, :, None] + update
        return ((new_top, total, acc), None)

    start_carry = (
        jnp.full((heads, rows), -1e30, jnp.float32),
        jnp.zeros((heads, rows), jnp.float32),
        jnp.zeros((heads, rows, HS), jnp.float32),
    )
    key = jnp.dot(normed, key_weight, preferred_element_type=jnp.float32).astype(jnp.bfloat16)
    value = jnp.dot(normed, value_weight, preferred_element_type=jnp.float32).astype(jnp.bfloat16)
    carry = start_carry
    keys = lax.all_gather(key, "blk", axis=0, tiled=True)
    values = lax.all_gather(value, "blk", axis=0, tiled=True)
    live_piece = lax.all_gather(counts, "blk", axis=0, tiled=True)
    shards = live_piece.shape[0]
    blocks = (keys.reshape(shards, rows, -1), values.reshape(shards, rows, -1), live_piece)
    carry, unused = lax.scan(attend_block, carry, blocks)
    top, total, acc = carry
    context = acc / total[:, :, None]
    context = context.transpose(1, 0, 2).reshape(rows, heads * HS).astype(jnp.bfloat16)
    own_stream = lax.dynamic_slice_in_dim(stream, head_place * half, half, 1)
    partial_out = jnp.dot(context, out_weight, preferred_element_type=jnp.float32)
    head_total = lax.psum_scatter(
        partial_out.astype(jnp.bfloat16), "head", scatter_dimension=1, tiled=True
    ).astype(jnp.float32)
    return (own_stream.astype(jnp.float32) + head_total).astype(jnp.bfloat16)


def solution(mesh):
    in_specs = (
        P(("sec", "blk"), None),
        P(("sec", "blk")),
        P(None, ("sec", "blk")),
        P(None, ("sec", "blk")),
        P(("sec", "blk")),
        P(None, "head"),
        P(),
        P(None, "head"),
        P(None, "head"),
        P(None, "head"),
        P("head", None),
    )
    out_specs = P(("sec", "blk"), "head")
    return jax.shard_map(local, mesh=mesh, in_specs=in_specs, out_specs=out_specs, check_vma=False)
```

profile of v0, /device:TPU:0, one launch (start us, length us, event | category | flops | bytes accessed | tf_op | source)
XLA Modules:
  0.0 282.3 jit_solution(9265060979988700921)
XLA Ops:
  6.5 3.0 %collective-permute-start = (bf16[512,768]{1,0:T(8,128)(2,1)}, bf16[512,768]{1,0:T(8,128)(2,1)S(1)}, u32[]{:S(2)}, u32[]{:S(2)}) collective-permute-start(bf16[512,768]{1,0:T(8,128)(2,1)} %param.13), channel_id=1, source_target_pairs={{0,2},{2,4},{4,6},{6,8},{8,10},{10,12},{12,14},{14,0},{1,3},{3,5},... | collective-permute-start | bytes 2359304 | tf_op jit(solution)/shard_map/ppermute | solution.py:16
  9.5 3.0 %collective-permute-start.1 = (bf16[512,768]{1,0:T(8,128)(2,1)}, bf16[512,768]{1,0:T(8,128)(2,1)}, u32[]{:S(2)}, u32[]{:S(2)}) collective-permute-start(bf16[512,768]{1,0:T(8,128)(2,1)} %param.13), channel_id=1, source_target_pairs={{2,0},{4,2},{6,4},{8,6},{10,8},{12,10},{14,12},{0,14},{3,1},{5,3},... | collective-permute-start | bytes 2359304 | tf_op jit(solution)/shard_map/ppermute | solution.py:17
  13.9 0.8 compare_select_fusion
  14.7 0.7 iota_compare_fusion.1
  15.4 28.1 %collective-permute-done = bf16[512,768]{1,0:T(8,128)(2,1)S(1)} collective-permute-done((bf16[512,768]{1,0:T(8,128)(2,1)}, bf16[512,768]{1,0:T(8,128)(2,1)S(1)}, u32[]{:S(2)}, u32[]{:S(2)}) %collective-permute-start) | collective-permute-done | bytes 786464 | tf_op jit(solution)/shard_map/ppermute | solution.py:16
  43.5 0.9 copy-done.2
  44.4 1.3 collective-permute-done.1
  45.7 1.8 pad_maximum_fusion
  47.4 13.6 %gather_fusion = bf16[3072,768]{1,0:T(8,128)(2,1)} fusion(bf16[1536,768]{1,0:T(8,128)(2,1)S(1)} %pad_maximum_fusion, s32[3072]{0:T(1024)S(1)} %broadcast_clamp_fusion), kind=kCustom, calls=%fused_computation | custom fusion | bytes 9449472 | tf_op jit(solution)/shard_map/gather | solution.py:49
  61.1 3.1 %convert_reduce_fusion = f32[512,768]{1,0:T(8,128)S(1)} fusion(bf16[6,512,768]{2,1,0:T(8,128)(2,1)} %bitcast.55, pred[6,512]{1,0:T(8,128)(4,1)S(1)} %iota_compare_fusion.1), kind=kLoop, calls=%fused_computation.23 | loop fusion | flops 6684672 | bytes 6294528 | tf_op jit(solution)/shard_map/reduce_sum | solution.py:52
  64.9 2.5 all_gather.12
  67.7 1.4 convolution_convert_fusion.1
  69.1 1.4 convolution_convert_fusion.3
  71.9 0.7 dynamic-update-slice
  72.6 11.3 %all-reduce = s32[8]{0:T(128)S(1)} all-reduce(s32[8]{0:T(128)S(1)} %dynamic-update-slice), channel_id=1, replica_groups=mesh['sec'=2,'blk'=8,'head'=2] {'blk'}, use_global_device_ids=true, to_apply=%add | all-reduce | flops 8 | bytes 64
  83.9 1.7 convolution_convert_fusion.2
  85.6 44.9 %all-gather.5.cloned.1.call-done = bf16[4096,384]{1,0:T(8,128)(2,1)} async-done(((bf16[512,384]{1,0:T(8,128)(2,1)}), bf16[4096,384]{1,0:T(8,128)(2,1)}) %all-gather.5.cloned.1.call-update) | async-done | bytes 3145744 | tf_op jit(solution)/shard_map/all_gather | solution.py:100
  130.5 61.3 %all-gather.3.cloned.1.call-done = bf16[4096,384]{1,0:T(8,128)(2,1)} async-done(((bf16[512,384]{1,0:T(8,128)(2,1)}), bf16[4096,384]{1,0:T(8,128)(2,1)}) %all-gather.3.cloned.1.call-update) | async-done | bytes 3145744 | tf_op jit(solution)/shard_map/all_gather | solution.py:99
  191.8 71.9 %while.15 = (s32[]{:T(128)}, f32[6,512]{1,0:T(8,128)S(1)}, f32[6,512]{1,0:T(8,128)S(1)}, f32[6,512,64]{1,2,0:T(8,128)}, s32[8]{0:T(128)S(1)}, /*index=5*/bf16[8,...) while((s32[]{:T(128)}, f32[6,512]{1,0:T(8,128)S(1)}, ...), condition=%wide.region_5.6_spmd.clone, body=%wide.region_2.5_spmd.clone.sunk | while | flops 423706112 | bytes 31262916 | solution.py:104
  193.1 1.2 constant_dynamic-slice_fusion.3
  194.7 1.6 bitcast_reduce_fusion.2
  196.2 1.9 fusion.45
  198.2 1.7 fusion.47
  199.9 0.9 copy-done.4
  202.0 1.2 constant_dynamic-slice_fusion.3
  203.6 1.6 bitcast_reduce_fusion.2
  205.2 1.9 fusion.45
  207.2 1.7 fusion.47
  208.9 0.9 copy-done.4
  211.0 1.2 constant_dynamic-slice_fusion.3
  212.6 1.6 bitcast_reduce_fusion.2
  214.2 1.9 fusion.45
  216.2 1.7 fusion.47
  217.9 0.9 copy-done.4
  220.0 1.2 constant_dynamic-slice_fusion.3
  221.6 1.6 bitcast_reduce_fusion.2
  223.2 1.9 fusion.45
  225.1 1.7 fusion.47
  226.9 0.9 copy-done.4
  229.0 1.2 constant_dynamic-slice_fusion.3
  230.6 1.6 bitcast_reduce_fusion.2
  232.2 1.9 fusion.45
  234.1 1.7 fusion.47
  235.9 0.9 copy-done.4
  238.0 1.2 constant_dynamic-slice_fusion.3
  239.6 1.6 bitcast_reduce_fusion.2
  241.2 1.9 fusion.45
  243.1 1.7 fusion.47
  244.9 0.9 copy-done.4
  247.0 1.2 constant_dynamic-slice_fusion.3
  248.6 1.6 bitcast_reduce_fusion.2
  250.1 1.9 fusion.45
  252.1 1.7 fusion.47
  253.8 0.9 copy-done.4
  255.9 1.2 constant_dynamic-slice_fusion.3
  257.5 1.6 bitcast_reduce_fusion.2
  259.1 1.9 fusion.45
  261.1 1.7 fusion.47
  262.8 0.9 copy-done.4
  263.7 1.2 divide_convert_fusion.1
  265.5 1.2 copy.19
  266.7 7.0 %reduce-scatter.4.cloned.1.call-done = bf16[384,512]{1,0:T(8,128)(2,1)} async-done(((bf16[768,512]{1,0:T(8,128)(2,1)}), bf16[384,512]{1,0:T(8,128)(2,1)}) %reduce-scatter.4.cloned.1.call-update) | async-done | bytes 393232
  273.8 1.2 copy.20
  275.0 0.8 add_convert_fusion
  (112 shorter events, 16.7 us)
Async XLA Ops:
  6.5 258.4 %copy-start = (bf16[384,768]{1,0:T(8,128)(2,1)S(1)}, bf16[384,768]{1,0:T(8,128)(2,1)}, u32[]{:S(2)}) copy-start(bf16[384,768]{1,0:T(8,128)(2,1)} %param.23) | copy-start | bytes 1769476
  6.5 124.0 %all-gather.5.cloned.1.call-start = ((), (), s32[]{:S(2)}) async-start(), calls=%async_computation.2 | async-start | bytes 3538944 | tf_op jit(solution)/shard_map/all_gather | solution.py:100
  6.5 36.9 %collective-permute-start = (bf16[512,768]{1,0:T(8,128)(2,1)}, bf16[512,768]{1,0:T(8,128)(2,1)S(1)}, u32[]{:S(2)}, u32[]{:S(2)}) collective-permute-start(bf16[512,768]{1,0:T(8,128)(2,1)} %param.13), channel_id=1, source_target_pairs={{0,2},{2,4},{4,6},{6,8},{8,10},{10,12},{12,14},{14,0},{1,3},{3,5},... | collective-permute-start | bytes 2359304 | tf_op jit(solution)/shard_map/ppermute | solution.py:16
  9.5 36.2 %collective-permute-start.1 = (bf16[512,768]{1,0:T(8,128)(2,1)}, bf16[512,768]{1,0:T(8,128)(2,1)}, u32[]{:S(2)}, u32[]{:S(2)}) collective-permute-start(bf16[512,768]{1,0:T(8,128)(2,1)} %param.13), channel_id=1, source_target_pairs={{2,0},{4,2},{6,4},{8,6},{10,8},{12,10},{14,12},{0,14},{3,1},{5,3},... | collective-permute-start | bytes 2359304 | tf_op jit(solution)/shard_map/ppermute | solution.py:17
  43.5 0.9 copy-start.2
  61.1 3.2 %copy-start.1 = (bf16[512,768]{1,0:T(8,128)(2,1)S(1)}, bf16[512,768]{1,0:T(8,128)(2,1)}, u32[]{:S(2)}) copy-start(bf16[512,768]{1,0:T(8,128)(2,1)} %param.13) | copy-start | bytes 2359300
  61.1 3.2 %copy-start.5 = (bf16[768,384]{1,0:T(8,128)(2,1)S(1)}, bf16[768,384]{1,0:T(8,128)(2,1)}, u32[]{:S(2)}) copy-start(bf16[768,384]{1,0:T(8,128)(2,1)} %param.18) | copy-start | bytes 1769476
  64.2 3.4 %copy-start.6 = (bf16[768,384]{1,0:T(8,128)(2,1)S(1)}, bf16[768,384]{1,0:T(8,128)(2,1)}, u32[]{:S(2)}) copy-start(bf16[768,384]{1,0:T(8,128)(2,1)} %param.22) | copy-start | bytes 1769476
  64.9 4.2 %copy-start.7 = (bf16[768,384]{1,0:T(8,128)(2,1)S(1)}, bf16[768,384]{1,0:T(8,128)(2,1)}, u32[]{:S(2)}) copy-start(bf16[768,384]{1,0:T(8,128)(2,1)} %param.21) | copy-start | bytes 1769476
  67.6 3.6 %copy-start.8 = (u32[32]{0:T(128)S(1)}, u32[32]{0:T(128)}, u32[]{:S(2)}) copy-start(u32[32]{0:T(128)} %constant.69) | copy-start | bytes 388
  69.1 122.7 %all-gather.3.cloned.1.call-start = ((), (), s32[]{:S(2)}) async-start(), calls=%async_computation.1 | async-start | bytes 3538944 | tf_op jit(solution)/shard_map/all_gather | solution.py:99
  70.5 203.2 %reduce-scatter.4.cloned.1.call-start = ((), (), s32[]{:S(2)}) async-start(), calls=%async_computation.3 | async-start | bytes 1179648
  196.2 1.9 copy-start.3
  199.9 0.9 copy-start.4
  205.2 1.9 copy-start.3
  208.9 0.9 copy-start.4
  214.2 1.9 copy-start.3
  217.9 0.9 copy-start.4
  223.2 1.9 copy-start.3
  226.9 0.9 copy-start.4
  232.2 1.9 copy-start.3
  235.8 0.9 copy-start.4
  241.2 1.9 copy-start.3
  244.8 0.9 copy-start.4
  250.1 1.9 copy-start.3
  253.8 0.9 copy-start.4
  259.1 1.9 copy-start.3
  262.8 0.9 copy-start.4
Sparse Core Ops, SparseCore 0:
  69.2 61.2 all-gather.4
  132.7 59.0 all-gather.2
  266.9 6.8 reduce-scatter.3
where the time goes:
time: 283 us; the launch traced here: 282 us
  waiting for transfers between devices  143 us (51%)
  local copies, waits for them, and re-layouts  42.6 us (15%)
  matrix products  31.8 us (11%)
  other arithmetic  30.6 us (11%)
  between operations  13.9 us (5%)
  blocking collectives  13.8 us (5%)
  starting transfers between devices  6.09 us (2%)
    all_gather x1, waiting for transfers between devices, local(): keys = lax.all_gather(key, 'blk', axis=0, tiled=True)  61.3 us
    all_gather x1, waiting for transfers between devices, local(): values = lax.all_gather(value, 'blk', axis=0, tiled=True)  44.9 us
    ppermute x1, waiting for transfers between devices, extended_2(): before = lax.ppermute(last, axis, up)  28.1 us
    dynamic_slice x32, local copies, waits for them, and re-layouts, local(): carry, unused = lax.scan(attend_block, carry, blocks)  17.3 us
    reduce_sum x8, other arithmetic, attend_block(): total = total * fade + jnp.sum(probs, axis=-1)  15.3 us
    dot_general x8, matrix products, attend_block(): jnp.einsum('hqk,khd->hqd', probs.astype(jnp.bfloat16), value_heads, prefe...  13.7 us
    gather x1, local copies, waits for them, and re-layouts, local(): picked = extended[local_rows]  13.6 us
    dot_general x8, matrix products, attend_block(): jnp.einsum('qhd,khd->hqk', query_heads, key_heads, preferred_element_type...  12.5 us
  transfers between devices with their start and end apart: 5, of which 5 were waited for; matrix products, arithmetic and copies ran while one was open for 3% of the time, Pallas kernels for 0%

commit v1 on v0

--- a/solution.py
+++ b/solution.py
@@ -4,6 +4,27 @@
 from jax.sharding import PartitionSpec as P
 
 HS = 64
+
+
+def collect(x, axis, dim):
+    peers, position, rows = (lax.axis_size(axis), lax.axis_index(axis), x.shape[dim])
+    upward = [(i, (i + 1) % peers) for i in range(peers)]
+    left = [(i, (i - 1) % peers) for i in range(peers)]
+    out = jnp.zeros((*x.shape[:dim], peers * rows, *x.shape[dim + 1 :]), x.dtype)
+    out = lax.dynamic_update_slice_in_dim(out, x, position * rows, axis=dim)
+    from_left = from_right = x
+    middle = peers // 2
+    for turn in range(1, middle + 1):
+        from_left = lax.ppermute(from_left, axis, upward)
+        out = lax.dynamic_update_slice_in_dim(
+            out, from_left, (position - turn) % peers * rows, axis=dim
+        )
+        if turn < peers - middle:
+            from_right = lax.ppermute(from_right, axis, left)
+            out = lax.dynamic_update_slice_in_dim(
+                out, from_right, (position + turn) % peers * rows, axis=dim
+            )
+    return out
 
 
 def extended_2(array, sides, width):
@@ -97,7 +118,7 @@
     value = jnp.dot(normed, value_weight, preferred_element_type=jnp.float32).astype(jnp.bfloat16)
     carry = start_carry
     keys = lax.all_gather(key, "blk", axis=0, tiled=True)
-    values = lax.all_gather(value, "blk", axis=0, tiled=True)
+    values = collect(value, "blk", 0)
     live_piece = lax.all_gather(counts, "blk", axis=0, tiled=True)
     shards = live_piece.shape[0]
     blocks = (keys.reshape(shards, rows, -1), values.reshape(shards, rows, -1), live_piece)

time: 283 us -> 260 us (0.919)
  waiting for transfers between devices: 143 us -> 84 us
  starting transfers between devices: 6.09 us -> 23.5 us
  blocking collectives: 13.8 us -> 24.1 us
  local copies, waits for them, and re-layouts: 42.6 us -> 49.2 us
    all_gather x1, waiting for transfers between devices: 61.3 us -> 0.01 us  [local(): keys = lax.all_gather(key, 'blk', axis=0, tiled=True)]
    ppermute x0 -> x7, waiting for transfers between devices: none -> 46.8 us  [the longest x4 45 us: collect(): from_left = lax.ppermute(from_left, axis, upward)]
    all_gather x1 -> x0, waiting for transfers between devices: 44.9 us -> none  [local(): values = lax.all_gather(value, 'blk', axis=0, tiled=True)]
    ppermute x0 -> x7, starting transfers between devices: none -> 17.5 us  [the longest x3 12.2 us: collect(): from_right = lax.ppermute(from_right, axis, left)]
    unnamed x1, blocking collectives: 11.3 us -> 21.8 us
    dynamic_update_slice x0 -> x7, local copies, waits for them, and re-layouts: none -> 5.55 us  [the longest x4 3.18 us: collect(): lax.dynamic_update_slice_in_dim(out, from_left, (position - turn) % peers...]
    unnamed x4 -> x3, waiting for transfers between devices: 7.07 us -> 6.92 us
  transfers between devices with their start and end apart: 5 -> 11, of which waited for: 5 -> 7; matrix products, arithmetic and copies ran while one was open for 3% -> 6% of each run, Pallas kernels for 0% -> 0%
where the time goes in v1:
time: 260 us; the launch traced here: 259 us
  waiting for transfers between devices  84 us (32%)
  local copies, waits for them, and re-layouts  49.2 us (19%)
  matrix products  32.9 us (13%)
  other arithmetic  30.6 us (12%)
  blocking collectives  24.1 us (9%)
  starting transfers between devices  23.5 us (9%)
  between operations  14.2 us (5%)
    ppermute x4, waiting for transfers between devices, collect(): from_left = lax.ppermute(from_left, axis, upward)  45 us
    ppermute x1, waiting for transfers between devices, extended_2(): before = lax.ppermute(last, axis, up)  28.1 us
    unnamed x1, blocking collectives  21.8 us
    dynamic_slice x32, local copies, waits for them, and re-layouts, local(): carry, unused = lax.scan(attend_block, carry, blocks)  17.3 us
    reduce_sum x8, other arithmetic, attend_block(): total = total * fade + jnp.sum(probs, axis=-1)  15.3 us
    dot_general x8, matrix products, attend_block(): jnp.einsum('hqk,khd->hqd', probs.astype(jnp.bfloat16), value_heads, prefe...  13.7 us
    gather x1, local copies, waits for them, and re-layouts, local(): picked = extended[local_rows]  13.6 us
    dot_general x8, matrix products, attend_block(): jnp.einsum('qhd,khd->hqk', query_heads, key_heads, preferred_element_type...  12.5 us
  transfers between devices with their start and end apart: 11, of which 7 were waited for; matrix products, arithmetic and copies ran while one was open for 6% of the time, Pallas kernels for 0%

profile of v1, /device:TPU:0, one launch (start us, length us, event | category | flops | bytes accessed | tf_op | source)
XLA Modules:
  0.0 259.3 jit_solution(13589350365326529704)
XLA Ops:
  6.5 3.0 %collective-permute-start = (bf16[512,768]{1,0:T(8,128)(2,1)}, bf16[512,768]{1,0:T(8,128)(2,1)}, u32[]{:S(2)}, u32[]{:S(2)}) collective-permute-start(bf16[512,768]{1,0:T(8,128)(2,1)} %param.13), channel_id=1, source_target_pairs={{0,2},{2,4},{4,6},{6,8},{8,10},{10,12},{12,14},{14,0},{1,3},{3,5},... | collective-permute-start | bytes 2359304 | tf_op jit(solution)/shard_map/ppermute | solution.py:37
  9.5 3.0 %collective-permute-start.1 = (bf16[512,768]{1,0:T(8,128)(2,1)}, bf16[512,768]{1,0:T(8,128)(2,1)}, u32[]{:S(2)}, u32[]{:S(2)}) collective-permute-start(bf16[512,768]{1,0:T(8,128)(2,1)} %param.13), channel_id=1, source_target_pairs={{2,0},{4,2},{6,4},{8,6},{10,8},{12,10},{14,12},{0,14},{3,1},{5,3},... | collective-permute-start | bytes 2359304 | tf_op jit(solution)/shard_map/ppermute | solution.py:38
  15.4 28.1 %collective-permute-done = bf16[512,768]{1,0:T(8,128)(2,1)} collective-permute-done((bf16[512,768]{1,0:T(8,128)(2,1)}, bf16[512,768]{1,0:T(8,128)(2,1)}, u32[]{:S(2)}, u32[]{:S(2)}) %collective-permute-start) | collective-permute-done | bytes 786464 | tf_op jit(solution)/shard_map/ppermute | solution.py:37
  43.5 2.2 collective-permute-done.1
  45.7 1.8 pad_maximum_fusion
  47.4 13.6 %gather_fusion = bf16[3072,768]{1,0:T(8,128)(2,1)} fusion(bf16[1536,768]{1,0:T(8,128)(2,1)S(1)} %pad_maximum_fusion, s32[3072]{0:T(1024)S(1)} %broadcast_clamp_fusion), kind=kCustom, calls=%fused_computation | custom fusion | bytes 9449472 | tf_op jit(solution)/shard_map/gather | solution.py:70
  61.0 3.1 %convert_reduce_fusion = f32[512,768]{1,0:T(8,128)S(1)} fusion(bf16[6,512,768]{2,1,0:T(8,128)(2,1)} %bitcast.55, pred[6,512]{1,0:T(8,128)(4,1)S(1)} %iota_compare_fusion.1), kind=kLoop, calls=%fused_computation.23 | loop fusion | flops 6684672 | bytes 6294528 | tf_op jit(solution)/shard_map/reduce_sum | solution.py:73
  64.8 2.4 all_gather.9
  67.5 1.4 convolution_convert_fusion.3
  68.9 2.0 broadcast_in_dim.63
  70.9 1.4 constant_dynamic-update-slice_fusion.7
  72.5 4.4 %collective-permute-start.3 = (bf16[512,384]{1,0:T(8,128)(2,1)S(1)}, bf16[512,384]{1,0:T(8,128)(2,1)S(1)}, u32[]{:S(2)}, u32[]{:S(2)}) collective-permute-start(bf16[512,384]{1,0:T(8,128)(2,1)S(1)} %get-tuple-element.124), channel_id=1, source_target_pairs={{0,14},{2,0},{4,2},{6,4},{8,6},{10,8},{12,10},{14,12},{1,15},{3,1}... | collective-permute-start | bytes 1179656 | tf_op jit(solution)/shard_map/ppermute | solution.py:23
  77.0 16.9 %collective-permute-done.2 = bf16[512,384]{1,0:T(8,128)(2,1)S(1)} collective-permute-done((bf16[512,384]{1,0:T(8,128)(2,1)S(1)}, bf16[512,384]{1,0:T(8,128)(2,1)S(1)}, u32[]{:S(2)}, u32[]{:S(2)}) %collective-permute-start.2) | collective-permute-done | bytes 393248 | tf_op jit(solution)/shard_map/ppermute | solution.py:18
  93.9 2.5 collective-permute-start.4
  98.4 3.0 %collective-permute-start.5 = (bf16[512,384]{1,0:T(8,128)(2,1)S(1)}, bf16[512,384]{1,0:T(8,128)(2,1)S(1)}, u32[]{:S(2)}, u32[]{:S(2)}) collective-permute-start(bf16[512,384]{1,0:T(8,128)(2,1)S(1)} %collective-permute-done.3), channel_id=1, source_target_pairs={{0,14},{2,0},{4,2},{6,4},{8,6},{10,8},{12,10},{14,12},{1,15},{3,1}... | collective-permute-start | bytes 1179656 | tf_op jit(solution)/shard_map/ppermute | solution.py:23
  101.4 21.8 %all-reduce = s32[8]{0:T(128)S(1)} all-reduce(s32[8]{0:T(128)S(1)} %dynamic-update-slice), channel_id=1, replica_groups=mesh['sec'=2,'blk'=8,'head'=2] {'blk'}, use_global_device_ids=true, to_apply=%add | all-reduce | flops 8 | bytes 64
  123.2 1.7 convolution_convert_fusion.2
  125.7 4.7 %collective-permute-start.7 = (bf16[512,384]{1,0:T(8,128)(2,1)S(1)}, bf16[512,384]{1,0:T(8,128)(2,1)S(1)}, u32[]{:S(2)}, u32[]{:S(2)}) collective-permute-start(bf16[512,384]{1,0:T(8,128)(2,1)S(1)} %collective-permute-done.5), channel_id=1, source_target_pairs={{0,14},{2,0},{4,2},{6,4},{8,6},{10,8},{12,10},{14,12},{1,15},{3,1}... | collective-permute-start | bytes 1179656 | tf_op jit(solution)/shard_map/ppermute | solution.py:23
  131.2 16.5 %collective-permute-done.6 = bf16[512,384]{1,0:T(8,128)(2,1)S(1)} collective-permute-done((bf16[512,384]{1,0:T(8,128)(2,1)S(1)}, bf16[512,384]{1,0:T(8,128)(2,1)S(1)}, u32[]{:S(2)}, u32[]{:S(2)}) %collective-permute-start.6) | collective-permute-done | bytes 393248 | tf_op jit(solution)/shard_map/ppermute | solution.py:18
  147.7 2.5 collective-permute-start.8
  152.6 1.8 collective-permute-done.7
  155.2 11.6 %collective-permute-done.8 = bf16[512,384]{1,0:T(8,128)(2,1)S(1)} collective-permute-done((bf16[512,384]{1,0:T(8,128)(2,1)S(1)}, bf16[512,384]{1,0:T(8,128)(2,1)S(1)}, u32[]{:S(2)}, u32[]{:S(2)}) %collective-permute-start.8) | collective-permute-done | bytes 393248 | tf_op jit(solution)/shard_map/ppermute | solution.py:18
  167.6 71.9 %while.15 = (s32[]{:T(128)}, f32[6,512]{1,0:T(8,128)S(1)}, f32[6,512]{1,0:T(8,128)S(1)}, f32[6,512,64]{1,2,0:T(8,128)}, s32[8]{0:T(128)S(1)}, /*index=5*/bf16[8,...) while((s32[]{:T(128)}, f32[6,512]{1,0:T(8,128)S(1)}, ...), condition=%wide.region_5.6_spmd.clone, body=%wide.region_2.5_spmd.clone.sunk | while | flops 423706112 | bytes 31262916 | solution.py:125
  168.8 1.2 constant_dynamic-slice_fusion.3
  170.4 1.6 bitcast_reduce_fusion.2
  172.0 1.9 fusion.45
  173.9 1.7 fusion.47
  175.7 0.9 copy-done.3
  177.8 1.2 constant_dynamic-slice_fusion.3
  179.4 1.6 bitcast_reduce_fusion.2
  181.0 1.9 fusion.45
  182.9 1.7 fusion.47
  186.8 1.2 constant_dynamic-slice_fusion.3
  188.4 1.6 bitcast_reduce_fusion.2
  190.0 1.9 fusion.45
  191.9 1.7 fusion.47
  193.7 0.9 copy-done.3
  195.8 1.2 constant_dynamic-slice_fusion.3
  197.4 1.6 bitcast_reduce_fusion.2
  199.0 1.9 fusion.45
  200.9 1.7 fusion.47
  204.8 1.2 constant_dynamic-slice_fusion.3
  206.4 1.6 bitcast_reduce_fusion.2
  208.0 1.9 fusion.45
  209.9 1.7 fusion.47
  211.6 0.9 copy-done.3
  213.8 1.2 constant_dynamic-slice_fusion.3
  215.4 1.6 bitcast_reduce_fusion.2
  216.9 1.9 fusion.45
  218.9 1.7 fusion.47
  222.7 1.2 constant_dynamic-slice_fusion.3
  224.3 1.6 bitcast_reduce_fusion.2
  225.9 1.9 fusion.45
  227.9 1.7 fusion.47
  229.6 0.9 copy-done.3
  231.7 1.2 constant_dynamic-slice_fusion.3
  233.3 1.6 bitcast_reduce_fusion.2
  234.9 1.9 fusion.45
  236.9 1.7 fusion.47
  239.5 1.2 divide_convert_fusion.1
  240.7 1.7 convolution_convert_fusion
  242.4 1.2 copy.21
  243.6 6.9 %reduce-scatter.4.cloned.1.call-done = bf16[384,512]{1,0:T(8,128)(2,1)} async-done(((bf16[768,512]{1,0:T(8,128)(2,1)}), bf16[384,512]{1,0:T(8,128)(2,1)}) %reduce-scatter.4.cloned.1.call-update) | async-done | bytes 393232
  250.4 1.2 copy.22
  (127 shorter events, 28.5 us)
Async XLA Ops:
  6.5 64.3 %copy-start = (bf16[768,384]{1,0:T(8,128)(2,1)S(1)}, bf16[768,384]{1,0:T(8,128)(2,1)}, u32[]{:S(2)}) copy-start(bf16[768,384]{1,0:T(8,128)(2,1)} %param.22) | copy-start | bytes 1769476
  6.5 161.0 %all-gather.2.cloned.1.call-start = ((), (), s32[]{:S(2)}) async-start(), calls=%async_computation.1 | async-start | bytes 3538944 | tf_op jit(solution)/shard_map/all_gather | solution.py:120
  6.5 36.9 %collective-permute-start = (bf16[512,768]{1,0:T(8,128)(2,1)}, bf16[512,768]{1,0:T(8,128)(2,1)}, u32[]{:S(2)}, u32[]{:S(2)}) collective-permute-start(bf16[512,768]{1,0:T(8,128)(2,1)} %param.13), channel_id=1, source_target_pairs={{0,2},{2,4},{4,6},{6,8},{8,10},{10,12},{12,14},{14,0},{1,3},{3,5},... | collective-permute-start | bytes 2359304 | tf_op jit(solution)/shard_map/ppermute | solution.py:37
  9.5 36.2 %collective-permute-start.1 = (bf16[512,768]{1,0:T(8,128)(2,1)}, bf16[512,768]{1,0:T(8,128)(2,1)}, u32[]{:S(2)}, u32[]{:S(2)}) collective-permute-start(bf16[512,768]{1,0:T(8,128)(2,1)} %param.13), channel_id=1, source_target_pairs={{2,0},{4,2},{6,4},{8,6},{10,8},{12,10},{14,12},{0,14},{3,1},{5,3},... | collective-permute-start | bytes 2359304 | tf_op jit(solution)/shard_map/ppermute | solution.py:38
  61.0 3.2 %copy-start.1 = (bf16[512,768]{1,0:T(8,128)(2,1)S(1)}, bf16[512,768]{1,0:T(8,128)(2,1)}, u32[]{:S(2)}) copy-start(bf16[512,768]{1,0:T(8,128)(2,1)} %param.13) | copy-start | bytes 2359300
  61.0 3.2 %copy-start.4 = (bf16[768,384]{1,0:T(8,128)(2,1)S(1)}, bf16[768,384]{1,0:T(8,128)(2,1)}, u32[]{:S(2)}) copy-start(bf16[768,384]{1,0:T(8,128)(2,1)} %param.18) | copy-start | bytes 1769476
  64.2 3.3 %copy-start.5 = (bf16[768,384]{1,0:T(8,128)(2,1)S(1)}, bf16[768,384]{1,0:T(8,128)(2,1)}, u32[]{:S(2)}) copy-start(bf16[768,384]{1,0:T(8,128)(2,1)} %param.21) | copy-start | bytes 1769476
  68.9 28.1 %copy-start.6 = (u32[32]{0:T(128)S(1)}, u32[32]{0:T(128)}, u32[]{:S(2)}) copy-start(u32[32]{0:T(128)} %constant.118) | copy-start | bytes 388
  68.9 181.6 %reduce-scatter.4.cloned.1.call-start = ((), (), s32[]{:S(2)}) async-start(), calls=%async_computation.2 | async-start | bytes 1179648
  72.2 21.6 %collective-permute-start.2 = (bf16[512,384]{1,0:T(8,128)(2,1)S(1)}, bf16[512,384]{1,0:T(8,128)(2,1)S(1)}, u32[]{:S(2)}, u32[]{:S(2)}) collective-permute-start(bf16[512,384]{1,0:T(8,128)(2,1)S(1)} %get-tuple-element.124), channel_id=1, source_target_pairs={{0,2},{2,4},{4,6},{6,8},{8,10},{10,12},{12,14},{14,0},{1,3},{3,5},... | collective-permute-start | bytes 1179656 | tf_op jit(solution)/shard_map/ppermute | solution.py:18
  72.5 25.8 %collective-permute-start.3 = (bf16[512,384]{1,0:T(8,128)(2,1)S(1)}, bf16[512,384]{1,0:T(8,128)(2,1)S(1)}, u32[]{:S(2)}, u32[]{:S(2)}) collective-permute-start(bf16[512,384]{1,0:T(8,128)(2,1)S(1)} %get-tuple-element.124), channel_id=1, source_target_pairs={{0,14},{2,0},{4,2},{6,4},{8,6},{10,8},{12,10},{14,12},{1,15},{3,1}... | collective-permute-start | bytes 1179656 | tf_op jit(solution)/shard_map/ppermute | solution.py:23
  93.9 29.3 %collective-permute-start.4 = (bf16[512,384]{1,0:T(8,128)(2,1)S(1)}, bf16[512,384]{1,0:T(8,128)(2,1)S(1)}, u32[]{:S(2)}, u32[]{:S(2)}) collective-permute-start(bf16[512,384]{1,0:T(8,128)(2,1)S(1)} %collective-permute-done.2), channel_id=1, source_target_pairs={{0,2},{2,4},{4,6},{6,8},{8,10},{10,12},{12,14},{14,0},{1,3},{3,5},... | collective-permute-start | bytes 1179656 | tf_op jit(solution)/shard_map/ppermute | solution.py:18
  98.4 27.4 %collective-permute-start.5 = (bf16[512,384]{1,0:T(8,128)(2,1)S(1)}, bf16[512,384]{1,0:T(8,128)(2,1)S(1)}, u32[]{:S(2)}, u32[]{:S(2)}) collective-permute-start(bf16[512,384]{1,0:T(8,128)(2,1)S(1)} %collective-permute-done.3), channel_id=1, source_target_pairs={{0,14},{2,0},{4,2},{6,4},{8,6},{10,8},{12,10},{14,12},{1,15},{3,1}... | collective-permute-start | bytes 1179656 | tf_op jit(solution)/shard_map/ppermute | solution.py:23
  123.2 24.6 %collective-permute-start.6 = (bf16[512,384]{1,0:T(8,128)(2,1)S(1)}, bf16[512,384]{1,0:T(8,128)(2,1)S(1)}, u32[]{:S(2)}, u32[]{:S(2)}) collective-permute-start(bf16[512,384]{1,0:T(8,128)(2,1)S(1)} %collective-permute-done.4), channel_id=1, source_target_pairs={{0,2},{2,4},{4,6},{6,8},{8,10},{10,12},{12,14},{14,0},{1,3},{3,5},... | collective-permute-start | bytes 1179656 | tf_op jit(solution)/shard_map/ppermute | solution.py:18
  125.7 28.7 %collective-permute-start.7 = (bf16[512,384]{1,0:T(8,128)(2,1)S(1)}, bf16[512,384]{1,0:T(8,128)(2,1)S(1)}, u32[]{:S(2)}, u32[]{:S(2)}) collective-permute-start(bf16[512,384]{1,0:T(8,128)(2,1)S(1)} %collective-permute-done.5), channel_id=1, source_target_pairs={{0,14},{2,0},{4,2},{6,4},{8,6},{10,8},{12,10},{14,12},{1,15},{3,1}... | collective-permute-start | bytes 1179656 | tf_op jit(solution)/shard_map/ppermute | solution.py:23
  147.7 19.0 %collective-permute-start.8 = (bf16[512,384]{1,0:T(8,128)(2,1)S(1)}, bf16[512,384]{1,0:T(8,128)(2,1)S(1)}, u32[]{:S(2)}, u32[]{:S(2)}) collective-permute-start(bf16[512,384]{1,0:T(8,128)(2,1)S(1)} %collective-permute-done.6), channel_id=1, source_target_pairs={{0,2},{2,4},{4,6},{6,8},{8,10},{10,12},{12,14},{14,0},{1,3},{3,5},... | collective-permute-start | bytes 1179656 | tf_op jit(solution)/shard_map/ppermute | solution.py:18
  172.0 1.9 copy-start.2
  175.7 0.9 copy-start.3
  181.0 1.9 copy-start.2
  184.7 0.9 copy-start.3
  190.0 1.9 copy-start.2
  193.6 0.9 copy-start.3
  199.0 1.9 copy-start.2
  202.6 0.9 copy-start.3
  207.9 1.9 copy-start.2
  211.6 0.9 copy-start.3
  216.9 1.9 copy-start.2
  220.6 0.9 copy-start.3
  225.9 1.9 copy-start.2
  229.6 0.9 copy-start.3
  234.9 1.9 copy-start.2
  238.6 0.9 copy-start.3
Sparse Core Ops, SparseCore 0:
  69.0 91.7 all-gather.1
  243.7 6.7 reduce-scatter.3
